TPU v7x, 32 devices: a whole 2x2x4 slice. The times are simulated.
32 devices in a mesh: grp: 2 (over y), seq: 4 (over z), col: 4 (over x, core).
Axes of the slice: x: 2, y: 2, z: 4, core: 2. Of those that a mesh axis runs over, the one named last changes fastest.
Arguments:
- tokens: bfloat16 [4096, 4608], P(('grp', 'seq'), 'col'), parts along dimension 0, may hold values from -14 to 14
- norm_gain: float32 [4608], replicated, may hold values from 0.5 to 1.5
- query_weight: bfloat16 [4608, 2048], P('seq', 'col'), may hold values from -1 to 1
- key_weight: bfloat16 [4608, 1024], P('seq', 'col'), may hold values from -1 to 1
- value_weight: bfloat16 [4608, 1024], P('seq', 'col'), may hold values from -0.09375 to 0.09375
- out_weight: bfloat16 [2048, 4608], P('seq', 'col'), may hold values from -1 to 1
- positions: int32 [4096], P(('grp', 'seq')), parts along dimension 0, may hold values from 0 to 2047, as said below
Outputs:
- block_out: bfloat16 [4096, 4608], P(('grp', 'seq'), 'col'), parts along dimension 0
There are 2 independent parts, one for each index of `grp`. A program takes and returns all parts, laid end to end along the dimension named above; an argument that names none is the same for every part. Nothing has to cross between parts.
Inputs may be any that keep to these rules, and one draw needn't show every extreme that they name: Within a document positions rise by one from token to token. Exactly one document starts inside the slab, at a token of its middle half, where positions restart at 0; the document before it ends at position 2047.
All inputs are finite; a program needn't handle non-finite values.
Results may differ from a plain program's by a relative error of at most 0.012.
The roundings to bfloat16 on the way count: a program that leaves them out, or rounds other values in their place, can miss the bound.
Values may be sent and summed in bfloat16 or wider, within the bound.
A program may use at most 64 MiB of HBM per device.

v0:
```python
import jax
import jax.numpy as jnp
from jax import lax
from jax.sharding import PartitionSpec as P

KVH = 8
HD = 128
WIN = 4096
score_scale = 1.0 / 12.0
rope_base = 10000.0


def passed_along(block, axis, distance):
    devices = range(lax.axis_size(axis))
    route = [(i - distance, i) for i in devices if i - distance in devices]
    return lax.ppermute(block, axis, route)


def rms_norm(values_in, norm_gain):
    floats = values_in.astype(jnp.float32)
    square_mean = jnp.mean(floats * floats, axis=-1, keepdims=True)
    return (floats * lax.rsqrt(square_mean + 1e-06) * norm_gain).astype(jnp.bfloat16)


def rotate(heads_in, places):
    width = heads_in.shape[-1]
    half = width // 2
    inverse = jnp.exp(-jnp.log(rope_base) * jnp.arange(half, dtype=jnp.float32) * (2.0 / width))
    angle = places.astype(jnp.float32)[:, None] * inverse[None, :]
    cosine = jnp.cos(angle)[:, None, :]
    sine = jnp.sin(angle)[:, None, :]
    lower = heads_in[..., :half]
    upper = heads_in[..., half:]
    return jnp.concatenate([lower * cosine - upper * sine, upper * cosine + lower * sine], axis=-1)


def per_device(tokens, norm_gain, query_weight, key_weight, value_weight, out_weight, positions):
    tok_rows = tokens.shape[0]
    col_count = lax.axis_size("col")
    seq_count = lax.axis_size("seq")
    seq_index = lax.axis_index("seq")
    kv_local = KVH // col_count
    whole = lax.all_gather(tokens, "col", axis=1, tiled=True)
    normed = rms_norm(whole, norm_gain)
    all_places = lax.all_gather(positions, "seq", axis=0, tiled=True)
    pieces = (
        lax.all_gather(query_weight, "seq", axis=0, tiled=True),
        lax.all_gather(key_weight, "seq", axis=0, tiled=True),
        lax.all_gather(value_weight, "seq", axis=0, tiled=True),
    )
    columns = normed
    query_raw, key_raw, value_raw = tuple(
        (jnp.dot(columns, piece, preferred_element_type=jnp.float32) for piece in pieces)
    )
    queries = (
        rotate(query_raw.reshape(tok_rows, 2 * kv_local, HD), positions)
        .astype(jnp.bfloat16)
        .reshape(tok_rows, kv_local, 2, HD)
    )
    keys = (
        rotate(key_raw.reshape(tok_rows, kv_local, HD), positions)
        .astype(jnp.bfloat16)
        .reshape(tok_rows, kv_local * HD)
    )
    values = value_raw.astype(jnp.bfloat16)
    packed = jnp.stack([keys, values])
    reach = min(WIN // tok_rows, seq_count - 1)
    blocks = [packed]
    current = packed
    for step in range(reach):
        current = passed_along(current, "seq", 1)
        blocks.insert(0, current)
    window = jnp.concatenate(blocks, axis=1)
    span = (reach + 1) * tok_rows
    places_pad = jnp.concatenate([jnp.zeros((reach * tok_rows,), jnp.int32), all_places], axis=0)
    key_places = lax.dynamic_slice_in_dim(places_pad, seq_index * tok_rows, span, 0)
    key_index = (seq_index - reach) * tok_rows + jnp.arange(span, dtype=jnp.int32)
    query_index = seq_index * tok_rows + jnp.arange(tok_rows, dtype=jnp.int32)
    group = 1
    for candidate in range(1, reach + 2):
        if (reach + 1) % candidate == 0 and candidate * tok_rows <= max(512, tok_rows):
            group = candidate
    key_rows = group * tok_rows
    key_blocks = span // key_rows
    keys_blocked = window[0].reshape(key_blocks, key_rows, kv_local, HD)[::-1]
    values_blocked = window[1].reshape(key_blocks, key_rows, kv_local, HD)[::-1]
    places_blocked = key_places.reshape(key_blocks, key_rows)[::-1]
    index_blocked = key_index.reshape(key_blocks, key_rows)[::-1]

    def attend(carry, block):
        largest, total, summed = carry
        key_part, value_part, place_part, index_part = block
        scores = (
            jnp.einsum("qgeh,kgh->qgek", queries, key_part, preferred_element_type=jnp.float32)
            * score_scale
        )
        distance = query_index[:, None] - index_part[None, :]
        visible = (index_part[None, :] >= 0) & (distance >= 0) & (distance < WIN)
        visible = visible & (positions[:, None] - place_part[None, :] == distance)
        scores = jnp.where(visible[:, None, None, :], scores, -1e30)
        newest = jnp.maximum(largest, jnp.max(scores, axis=-1))
        factor = jnp.exp(largest - newest)
        weights = jnp.exp(scores - newest[..., None])
        total = total * factor + jnp.sum(weights, axis=-1)
        summed = summed * factor[..., None] + jnp.einsum(
            "qgek,kgh->qgeh",
            weights.astype(jnp.bfloat16),
            value_part,
            preferred_element_type=jnp.float32,
        )
        return ((newest, total, summed), None)

    start_state = (
        jnp.full((tok_rows, kv_local, 2), -1e30, jnp.float32),
        jnp.zeros((tok_rows, kv_local, 2), jnp.float32),
        jnp.zeros((tok_rows, kv_local, 2, HD), jnp.float32),
    )
    final_state, unused = lax.scan(
        attend, start_state, (keys_blocked, values_blocked, places_blocked, index_blocked)
    )
    attended = (
        (final_state[2] / final_state[1][..., None])
        .astype(jnp.bfloat16)
        .reshape(tok_rows, 2 * kv_local * HD)
    )
    mixed = lax.all_gather(attended, "col", axis=1, tiled=True)
    columns = mixed
    projected = jnp.dot(
        columns,
        lax.all_gather(out_weight, "seq", axis=0, tiled=True),
        preferred_element_type=jnp.float32,
    )
    return (tokens.astype(jnp.float32) + projected).astype(jnp.bfloat16)


def solution(mesh):
    return jax.shard_map(
        per_device,
        mesh=mesh,
        in_specs=(
            P(("grp", "seq"), "col"),
            P(),
            P("seq", "col"),
            P("seq", "col"),
            P("seq", "col"),
            P("seq", "col"),
            P(("grp", "seq")),
        ),
        out_specs=P(("grp", "seq"), "col"),
        check_vma=False,
    )
```

profile of v0, /device:TPU:0, one launch (start us, length us, event | category | flops | bytes accessed | tf_op | source)
XLA Modules:
  0.0 397.1 jit_solution(13647404061947721689)
XLA Ops:
  6.5 0.7 all-gather.8.cloned.1.call-update
  7.3 0.7 all-gather.10.cloned.1.call-update
  8.1 0.7 all-gather.12.cloned.1.call-update
  8.8 0.5 all-gather.14.cloned.1.call-update
  9.4 0.7 convert_element_type.41
  10.1 0.5 multiply_cosine_fusion
  10.6 38.5 %all-gather.8.cloned.1.call-done = bf16[512,4608]{1,0:T(8,128)(2,1)} async-done(((bf16[512,1152]{1,0:T(8,128)(2,1)}), bf16[512,4608]{1,0:T(8,128)(2,1)}) %all-gather.8.cloned.1.call-update) | async-done | bytes 4718608 | tf_op jit(solution)/shard_map/all_gather | solution.py:43
  49.1 3.3 fusion.31
  52.4 48.7 %all-gather.10.cloned.1.call-done = bf16[4608,256]{1,0:T(8,128)(2,1)} async-done(((bf16[1152,256]{1,0:T(8,128)(2,1)}), bf16[4608,256]{1,0:T(8,128)(2,1)}) %all-gather.10.cloned.1.call-update) | async-done | bytes 2359312 | tf_op jit(solution)/shard_map/all_gather | solution.py:48
  101.2 4.8 %fusion.39 = f32[512,256]{0,1:T(8,128)S(1)} fusion(bf16[4608,256]{1,0:T(8,128)(2,1)} %all-gather.10.cloned.1.call-done, bf16[512,4608]{1,0:T(8,128)(2,1)} %all-gather.8.cloned.1.call-done, f32[4608]{0:T(1024)S(1)} %copy-done.5, f32[512]{0:T(512)S(1)} %add_rsqrt_fusion), kind=kOutput, calls=%fused_computation.64 | convolution fusion | flops 1217396736 | bytes 7622656 | tf_op jit(solution)/shard_map/dot_general | solution.py:53
  106.3 45.8 %all-gather.12.cloned.1.call-done = bf16[4608,256]{1,0:T(8,128)(2,1)} async-done(((bf16[1152,256]{1,0:T(8,128)(2,1)}), bf16[4608,256]{1,0:T(8,128)(2,1)}) %all-gather.12.cloned.1.call-update) | async-done | bytes 2359312 | tf_op jit(solution)/shard_map/all_gather | solution.py:49
  152.1 4.6 %fusion.35 = bf16[1,512,256]{2,1,0:T(8,128)(2,1)S(1)} fusion(bf16[4608,256]{1,0:T(8,128)(2,1)} %all-gather.12.cloned.1.call-done, bf16[512,4608]{1,0:T(8,128)(2,1)} %all-gather.8.cloned.1.call-done, f32[4608]{0:T(1024)S(1)} %copy-done.5, f32[512]{0:T(512)S(1)} %add_rsqrt_fusion), kind=kOutput, calls=%fused_computation.47 | convolution fusion | flops 1217527808 | bytes 7360512 | tf_op jit(solution)/shard_map/dot_general | solution.py:53
  156.7 1.8 collective-permute-start
  158.5 20.3 %collective-permute-done = bf16[2,512,256]{2,1,0:T(8,128)(2,1)S(1)} collective-permute-done((bf16[2,512,256]{2,1,0:T(8,128)(2,1)S(1)}, bf16[2,512,256]{2,1,0:T(8,128)(2,1)S(1)}, u32[]{:S(2)}, u32[]{:S(2)}) %collective-permute-start) | collective-permute-done | bytes 524320 | tf_op jit(solution)/shard_map/ppermute | solution.py:16
  178.9 13.4 %collective-permute-start.1 = (bf16[2,512,256]{2,1,0:T(8,128)(2,1)S(1)}, bf16[2,512,256]{2,1,0:T(8,128)(2,1)S(1)}, u32[]{:S(2)}, u32[]{:S(2)}) collective-permute-start(bf16[2,512,256]{2,1,0:T(8,128)(2,1)S(1)} %collective-permute-done), channel_id=1, source_target_pairs={{0,4},{4,8},{8,12},{1,5},{5,9},{9,13},{2,6},{6,10},{10,14},{3,7},{... | collective-permute-start | bytes 1572872 | tf_op jit(solution)/shard_map/ppermute | solution.py:16
  192.4 45.2 %all-gather = s32[4,1,512]{2,1,0:T(1,128)S(1)} all-gather(s32[1,1,512]{2,1,0:T(1,128)S(1)} %bitcast.75), channel_id=1, replica_groups=mesh['grp'=2,'seq'=4,'col'=4] {'seq'}, dimensions={0}, use_global_device_ids=true | all-gather | bytes 10240 | tf_op jit(solution)/shard_map/all_gather | solution.py:45
  237.7 1.2 rev.13
  239.0 0.6 broadcast_add_fusion
  239.6 2.1 collective-permute-start.2
  241.8 26.4 %all-gather.14.cloned.1.call-done = bf16[4608,512]{1,0:T(8,128)(2,1)} async-done(((bf16[1152,512]{1,0:T(8,128)(2,1)}), bf16[4608,512]{1,0:T(8,128)(2,1)}) %all-gather.14.cloned.1.call-update) | async-done | bytes 4718608 | tf_op jit(solution)/shard_map/all_gather | solution.py:47
  268.2 6.9 %fusion.36 = f32[512,512]{0,1:T(8,128)S(1)} fusion(bf16[4608,512]{1,0:T(8,128)(2,1)} %all-gather.14.cloned.1.call-done, bf16[512,4608]{1,0:T(8,128)(2,1)} %all-gather.8.cloned.1.call-done, f32[4608]{0:T(1024)S(1)} %copy-done.5, f32[512]{0:T(512)S(1)} %add_rsqrt_fusion), kind=kOutput, calls=%fused_computation.63 | convolution fusion | flops 2425356288 | bytes 10506240 | tf_op jit(solution)/shard_map/dot_general | solution.py:53
  275.1 0.2 subtract_convert_fusion
  275.3 0.3 copy.17
  275.5 0.3 copy.18
  275.8 0.3 pad_maximum_fusion.1
  276.1 1.4 maximum_maximum_fusion
  277.5 1.1 fusion.41
  278.6 0.3 reshape_squeeze.6
  279.1 1.5 reshape_squeeze.7
  280.6 2.0 copy.19
  282.6 2.2 rev.15
  284.8 47.7 %while.15 = (s32[]{:T(128)}, f32[512,2,2]{0,2,1:T(2,128)S(1)}, f32[512,2,2]{0,2,1:T(2,128)S(1)}, f32[512,2,2,128]{0,3,2,1:T(8,128)}, s32[4,512]{1,0:T(4,128)}, /...) while((s32[]{:T(128)}, f32[512,2,2]{0,2,1:T(2,128)S(1)}, ...), condition=%wide.region_4.5_spmd.clone, body=%wide.region_1.4_spmd.clone.sunk | while | flops 551300096 | bytes 33705652 | solution.py:118
  284.9 0.8 compare_reduce_fusion.2
  285.7 0.7 constant_dynamic-slice_fusion.4
  286.4 0.5 fusion.60
  286.9 2.9 fusion.61
  289.8 3.3 fusion.63
  293.1 0.2 copy-done
  293.3 3.3 fusion.65
  296.6 0.7 compare_reduce_fusion.2
  297.3 0.7 constant_dynamic-slice_fusion.4
  298.0 0.5 fusion.60
  298.6 2.9 fusion.61
  301.4 3.3 fusion.63
  304.7 0.2 copy-done
  304.9 3.7 fusion.65
  308.6 0.7 compare_reduce_fusion.2
  309.3 0.7 constant_dynamic-slice_fusion.4
  310.0 0.5 fusion.60
  310.6 2.9 fusion.61
  313.4 3.3 fusion.63
  316.7 0.2 copy-done
  316.9 3.7 fusion.65
  320.6 0.7 compare_reduce_fusion.2
  321.3 0.7 constant_dynamic-slice_fusion.4
  322.0 0.5 fusion.60
  322.5 2.9 fusion.61
  325.4 3.3 fusion.63
  328.7 0.2 copy-done
  328.9 3.7 fusion.65
  332.6 2.1 divide_convert_fusion
  334.8 26.1 %all-gather.18.cloned.1.call-done = bf16[2048,1152]{1,0:T(8,128)(2,1)} async-done(((bf16[512,1152]{1,0:T(8,128)(2,1)}), bf16[2048,1152]{1,0:T(8,128)(2,1)}) %all-gather.18.cloned.1.call-update) | async-done | bytes 4718608 | tf_op jit(solution)/shard_map/all_gather | solution.py:130
  360.8 22.5 %all-gather.16.cloned.1.call-done = bf16[512,2048]{0,1:T(8,128)(2,1)} async-done(((bf16[512,512]{0,1:T(8,128)(2,1)}), bf16[512,2048]{0,1:T(8,128)(2,1)}) %all-gather.16.cloned.1.call-update) | async-done | bytes 2097168 | tf_op jit(solution)/shard_map/all_gather | solution.py:126
  383.3 6.9 %fusion.34 = bf16[512,1152]{1,0:T(8,128)(2,1)} fusion(bf16[512,2048]{0,1:T(8,128)(2,1)} %all-gather.16.cloned.1.call-done, bf16[2048,1152]{1,0:T(8,128)(2,1)} %all-gather.18.cloned.1.call-done, bf16[512,1152]{1,0:T(8,128)(2,1)S(1)} %copy-done.1), kind=kOutput, calls=%fused_computation.44 | convolution fusion | flops 2417688576 | bytes 9175040 | tf_op jit(solution)/shard_map/dot_general | solution.py:128
  (55 shorter events, 1.1 us)
Async XLA Ops:
  6.5 42.6 %all-gather.8.cloned.1.call-start = ((), (), s32[]{:S(2)}) async-start(), calls=%async_computation | async-start | bytes 5898240 | tf_op jit(solution)/shard_map/all_gather | solution.py:43
  6.5 94.6 %copy-start.5 = (f32[4608]{0:T(1024)S(1)}, f32[4608]{0:T(1024)}, u32[]{:S(2)}) copy-start(f32[4608]{0:T(1024)} %param.10) | copy-start | bytes 55300
  7.3 93.9 %all-gather.10.cloned.1.call-start = ((), (), s32[]{:S(2)}) async-start(), calls=%async_computation.1 | async-start | bytes 2949120 | tf_op jit(solution)/shard_map/all_gather | solution.py:48
  8.0 144.1 %all-gather.12.cloned.1.call-start = ((), (), s32[]{:S(2)}) async-start(), calls=%async_computation.2 | async-start | bytes 2949120 | tf_op jit(solution)/shard_map/all_gather | solution.py:49
  8.7 259.4 %all-gather.14.cloned.1.call-start = ((), (), s32[]{:S(2)}) async-start(), calls=%async_computation.3 | async-start | bytes 5898240 | tf_op jit(solution)/shard_map/all_gather | solution.py:47
  9.3 351.5 %all-gather.18.cloned.1.call-start = ((), (), s32[]{:S(2)}) async-start(), calls=%async_computation.5 | async-start | bytes 5898240 | tf_op jit(solution)/shard_map/all_gather | solution.py:130
  106.3 86.1 %copy-start.3 = (s32[512]{0:T(512)S(1)}, s32[512]{0:T(512)}, u32[]{:S(2)}) copy-start(s32[512]{0:T(512)} %param.15) | copy-start | bytes 6148
  156.7 22.1 %collective-permute-start = (bf16[2,512,256]{2,1,0:T(8,128)(2,1)S(1)}, bf16[2,512,256]{2,1,0:T(8,128)(2,1)S(1)}, u32[]{:S(2)}, u32[]{:S(2)}) collective-permute-start(bf16[2,512,256]{2,1,0:T(8,128)(2,1)S(1)} %pad_maximum_fusion), channel_id=1, source_target_pairs={{0,4},{4,8},{8,12},{1,5},{5,9},{9,13},{2,6},{6,10},{10,14},{3,7},{... | collective-permute-start | bytes 1572872 | tf_op jit(solution)/shard_map/ppermute | solution.py:16
  178.9 60.8 %collective-permute-start.1 = (bf16[2,512,256]{2,1,0:T(8,128)(2,1)S(1)}, bf16[2,512,256]{2,1,0:T(8,128)(2,1)S(1)}, u32[]{:S(2)}, u32[]{:S(2)}) collective-permute-start(bf16[2,512,256]{2,1,0:T(8,128)(2,1)S(1)} %collective-permute-done), channel_id=1, source_target_pairs={{0,4},{4,8},{8,12},{1,5},{5,9},{9,13},{2,6},{6,10},{10,14},{3,7},{... | collective-permute-start | bytes 1572872 | tf_op jit(solution)/shard_map/ppermute | solution.py:16
  192.3 191.0 %all-gather.16.cloned.1.call-start = ((), (), s32[]{:S(2)}) async-start(), calls=%async_computation.4 | async-start | bytes 2621440 | tf_op jit(solution)/shard_map/all_gather | solution.py:126
  239.6 36.5 %collective-permute-start.2 = (bf16[2,512,256]{2,1,0:T(8,128)(2,1)S(1)}, bf16[2,512,256]{2,1,0:T(8,128)(2,1)}, u32[]{:S(2)}, u32[]{:S(2)}) collective-permute-start(bf16[2,512,256]{2,1,0:T(8,128)(2,1)S(1)} %collective-permute-done.1), channel_id=1, source_target_pairs={{0,4},{4,8},{8,12},{1,5},{5,9},{9,13},{2,6},{6,10},{10,14},{3,7},{... | collective-permute-start | bytes 1572872 | tf_op jit(solution)/shard_map/ppermute | solution.py:16
  279.0 5.8 %copy-start.2 = (f32[512,2,2]{0,2,1:T(2,128)S(1)}, f32[512,2,2]{0,2,1:T(2,128)}, u32[]{:S(2)}) copy-start(f32[512,2,2]{0,2,1:T(2,128)} %custom-call.1) | copy-start | bytes 24580
  279.1 5.8 %copy-start.4 = (s32[512]{0:T(512)S(1)}, s32[512]{0:T(512)}, u32[]{:S(2)}) copy-start(s32[512]{0:T(512)} %param.15) | copy-start | bytes 6148
  284.8 98.5 %copy-start.1 = (bf16[512,1152]{1,0:T(8,128)(2,1)S(1)}, bf16[512,1152]{1,0:T(8,128)(2,1)}, u32[]{:S(2)}) copy-start(bf16[512,1152]{1,0:T(8,128)(2,1)} %param.9) | copy-start | bytes 3538948
  289.8 3.5 copy-start
  301.4 3.4 copy-start
  313.4 3.5 copy-start
  325.4 3.5 copy-start
Sparse Core Ops, SparseCore 0:
  8.9 40.1 all-gather.7
  50.7 50.4 all-gather.9
  102.8 49.2 all-gather.11
  153.5 114.6 all-gather.13
  269.6 91.2 all-gather.17
  362.3 21.0 all-gather.15
where the time goes:
time: 398 us; the launch traced here: 397 us
  waiting for transfers between devices  231 us (58%)
  matrix products  49.1 us (12%)
  blocking collectives  45.2 us (11%)
  other arithmetic  27.5 us (7%)
  starting transfers between devices  17.5 us (4%)
  between operations  13.7 us (3%)
  local copies, waits for them, and re-layouts  12.9 us (3%)
    all_gather x1, waiting for transfers between devices, per_device(): lax.all_gather(key_weight, 'seq', axis=0, tiled=True)  48.7 us
    all_gather x1, waiting for transfers between devices, per_device(): lax.all_gather(value_weight, 'seq', axis=0, tiled=True)  45.8 us
    all_gather x1, blocking collectives, per_device(): all_places = lax.all_gather(positions, 'seq', axis=0, tiled=True)  45.2 us
    all_gather x1, waiting for transfers between devices, per_device(): whole = lax.all_gather(tokens, 'col', axis=1, tiled=True)  38.5 us
    all_gather x1, waiting for transfers between devices, per_device(): lax.all_gather(query_weight, 'seq', axis=0, tiled=True)  26.4 us
    all_gather x1, waiting for transfers between devices, per_device(): lax.all_gather(out_weight, 'seq', axis=0, tiled=True)  26.1 us
    all_gather x1, waiting for transfers between devices, per_device(): mixed = lax.all_gather(attended, 'col', axis=1, tiled=True)  22.5 us
    ppermute x3, waiting for transfers between devices, passed_along(): return lax.ppermute(block, axis, route)  20.3 us
  transfers between devices with their start and end apart: 9, of which 7 were waited for; matrix products, arithmetic and copies ran while one was open for 21% of the time, Pallas kernels for 0%

commit v1 on v0

--- a/solution.py
+++ b/solution.py
@@ -123,7 +123,12 @@
         .astype(jnp.bfloat16)
         .reshape(tok_rows, 2 * kv_local * HD)
     )
-    mixed = lax.all_gather(attended, "col", axis=1, tiled=True)
+    ring = [attended]
+    for hop in range(3):
+        ring.append(lax.ppermute(ring[-1], "col", [(dev, (dev + 1) % 4) for dev in range(4)]))
+    mixed = jnp.roll(
+        jnp.concatenate(ring[::-1], axis=1), (lax.axis_index("col") + 1) * ring[0].shape[1], axis=1
+    )
     columns = mixed
     projected = jnp.dot(
         columns,

time: 398 us -> 376 us (0.945)
  waiting for transfers between devices: 231 us -> 211 us
  local copies, waits for them, and re-layouts: 12.9 us -> 19.6 us
  matrix products: 49.1 us -> 44.6 us
  other arithmetic: 27.5 us -> 23.3 us
    ppermute x0 -> x3, waiting for transfers between devices: none -> 25.7 us  [per_device(): lax.ppermute(ring[-1], 'col', [(dev, (dev + 1) % 4) for dev in range(4)])]
    all_gather x1, waiting for transfers between devices: 26.1 us -> 1.1 us  [per_device(): lax.all_gather(out_weight, 'seq', axis=0, tiled=True)]
    all_gather x1 -> x0, waiting for transfers between devices: 22.5 us -> none  [per_device(): mixed = lax.all_gather(attended, 'col', axis=1, tiled=True)]
    unnamed x10 -> x13, local copies, waits for them, and re-layouts: 0.02 us -> 5.86 us
    dot_general x4, matrix products: 14.5 us -> 9.94 us  [attend(): jnp.einsum('qgek,kgh->qgeh', weights.astype(jnp.bfloat16), value_part, pr...]
  transfers between devices with their start and end apart: 9 -> 11, of which waited for: 7 -> 9; matrix products, arithmetic and copies ran while one was open for 21% -> 20% of each run, Pallas kernels for 0% -> 0%
where the time goes in v1:
time: 376 us; the launch traced here: 375 us
  waiting for transfers between devices  211 us (56%)
  blocking collectives  45.3 us (12%)
  matrix products  44.6 us (12%)
  other arithmetic  23.3 us (6%)
  local copies, waits for them, and re-layouts  19.6 us (5%)
  starting transfers between devices  17.7 us (5%)
  between operations  13.4 us (4%)
    all_gather x1, waiting for transfers between devices, per_device(): lax.all_gather(key_weight, 'seq', axis=0, tiled=True)  48.7 us
    all_gather x1, waiting for transfers between devices, per_device(): lax.all_gather(value_weight, 'seq', axis=0, tiled=True)  45.8 us
    all_gather x1, blocking collectives, per_device(): all_places = lax.all_gather(positions, 'seq', axis=0, tiled=True)  45.3 us
    all_gather x1, waiting for transfers between devices, per_device(): whole = lax.all_gather(tokens, 'col', axis=1, tiled=True)  38.5 us
    all_gather x1, waiting for transfers between devices, per_device(): lax.all_gather(query_weight, 'seq', axis=0, tiled=True)  28.1 us
    ppermute x3, waiting for transfers between devices, per_device(): lax.ppermute(ring[-1], 'col', [(dev, (dev + 1) % 4) for dev in range(4)])  25.7 us
    ppermute x3, waiting for transfers between devices, passed_along(): return lax.ppermute(block, axis, route)  20.3 us
    ppermute x3, starting transfers between devices, passed_along(): return lax.ppermute(block, axis, route)  17.3 us
  transfers between devices with their start and end apart: 11, of which 9 were waited for; matrix products, arithmetic and copies ran while one was open for 20% of the time, Pallas kernels for 0%

profile of v1, /device:TPU:0, one launch (start us, length us, event | category | flops | bytes accessed | tf_op | source)
XLA Modules:
  0.0 375.0 jit_solution(3238544579781951162)
XLA Ops:
  6.5 0.7 all-gather.7.cloned.1.call-update
  7.3 0.7 all-gather.9.cloned.1.call-update
  8.1 0.7 all-gather.11.cloned.1.call-update
  8.8 0.5 all-gather.13.cloned.1.call-update
  9.4 0.7 convert_element_type.41
  10.1 0.5 multiply_cosine_fusion
  10.6 38.5 %all-gather.7.cloned.1.call-done = bf16[512,4608]{1,0:T(8,128)(2,1)} async-done(((bf16[512,1152]{1,0:T(8,128)(2,1)}), bf16[512,4608]{1,0:T(8,128)(2,1)}) %all-gather.7.cloned.1.call-update) | async-done | bytes 4718608 | tf_op jit(solution)/shard_map/all_gather | solution.py:43
  49.1 3.3 fusion.31
  52.4 48.7 %all-gather.9.cloned.1.call-done = bf16[4608,256]{1,0:T(8,128)(2,1)} async-done(((bf16[1152,256]{1,0:T(8,128)(2,1)}), bf16[4608,256]{1,0:T(8,128)(2,1)}) %all-gather.9.cloned.1.call-update) | async-done | bytes 2359312 | tf_op jit(solution)/shard_map/all_gather | solution.py:48
  101.2 4.8 %fusion.41 = f32[512,256]{0,1:T(8,128)S(1)} fusion(bf16[4608,256]{1,0:T(8,128)(2,1)} %all-gather.9.cloned.1.call-done, bf16[512,4608]{1,0:T(8,128)(2,1)} %all-gather.7.cloned.1.call-done, f32[4608]{0:T(1024)S(1)} %copy-done.5, f32[512]{0:T(512)S(1)} %add_rsqrt_fusion), kind=kOutput, calls=%fused_computation.74 | convolution fusion | flops 1217396736 | bytes 7622656 | tf_op jit(solution)/shard_map/dot_general | solution.py:53
  106.3 45.8 %all-gather.11.cloned.1.call-done = bf16[4608,256]{1,0:T(8,128)(2,1)} async-done(((bf16[1152,256]{1,0:T(8,128)(2,1)}), bf16[4608,256]{1,0:T(8,128)(2,1)}) %all-gather.11.cloned.1.call-update) | async-done | bytes 2359312 | tf_op jit(solution)/shard_map/all_gather | solution.py:49
  152.1 4.6 %fusion.36 = bf16[1,512,256]{2,1,0:T(8,128)(2,1)S(1)} fusion(bf16[4608,256]{1,0:T(8,128)(2,1)} %all-gather.11.cloned.1.call-done, bf16[512,4608]{1,0:T(8,128)(2,1)} %all-gather.7.cloned.1.call-done, f32[4608]{0:T(1024)S(1)} %copy-done.5, f32[512]{0:T(512)S(1)} %add_rsqrt_fusion), kind=kOutput, calls=%fused_computation.48 | convolution fusion | flops 1217527808 | bytes 7360512 | tf_op jit(solution)/shard_map/dot_general | solution.py:53
  156.7 1.8 collective-permute-start
  158.5 20.3 %collective-permute-done = bf16[2,512,256]{2,1,0:T(8,128)(2,1)S(1)} collective-permute-done((bf16[2,512,256]{2,1,0:T(8,128)(2,1)S(1)}, bf16[2,512,256]{2,1,0:T(8,128)(2,1)S(1)}, u32[]{:S(2)}, u32[]{:S(2)}) %collective-permute-start) | collective-permute-done | bytes 524320 | tf_op jit(solution)/shard_map/ppermute | solution.py:16
  178.9 13.4 %collective-permute-start.1 = (bf16[2,512,256]{2,1,0:T(8,128)(2,1)S(1)}, bf16[2,512,256]{2,1,0:T(8,128)(2,1)S(1)}, u32[]{:S(2)}, u32[]{:S(2)}) collective-permute-start(bf16[2,512,256]{2,1,0:T(8,128)(2,1)S(1)} %collective-permute-done), channel_id=1, source_target_pairs={{0,4},{4,8},{8,12},{1,5},{5,9},{9,13},{2,6},{6,10},{10,14},{3,7},{... | collective-permute-start | bytes 1572872 | tf_op jit(solution)/shard_map/ppermute | solution.py:16
  192.3 45.3 %all-gather = s32[4,1,512]{2,1,0:T(1,128)S(1)} all-gather(s32[1,1,512]{2,1,0:T(1,128)S(1)} %bitcast.76), channel_id=1, replica_groups=mesh['grp'=2,'seq'=4,'col'=4] {'seq'}, dimensions={0}, use_global_device_ids=true | all-gather | bytes 10240 | tf_op jit(solution)/shard_map/all_gather | solution.py:45
  238.0 2.1 collective-permute-start.2
  240.1 28.1 %all-gather.13.cloned.1.call-done = bf16[4608,512]{1,0:T(8,128)(2,1)} async-done(((bf16[1152,512]{1,0:T(8,128)(2,1)}), bf16[4608,512]{1,0:T(8,128)(2,1)}) %all-gather.13.cloned.1.call-update) | async-done | bytes 4718608 | tf_op jit(solution)/shard_map/all_gather | solution.py:47
  268.2 6.9 %fusion.38 = f32[512,512]{0,1:T(8,128)S(1)} fusion(bf16[4608,512]{1,0:T(8,128)(2,1)} %all-gather.13.cloned.1.call-done, bf16[512,4608]{1,0:T(8,128)(2,1)} %all-gather.7.cloned.1.call-done, f32[4608]{0:T(1024)S(1)} %copy-done.5, f32[512]{0:T(512)S(1)} %add_rsqrt_fusion), kind=kOutput, calls=%fused_computation.73 | convolution fusion | flops 2425356288 | bytes 10506240 | tf_op jit(solution)/shard_map/dot_general | solution.py:53
  275.3 0.3 copy.17
  275.6 0.3 copy.18
  275.9 0.3 pad_maximum_fusion.1
  276.2 1.4 maximum_maximum_fusion
  277.5 1.1 fusion.43
  278.7 0.3 reshape_squeeze.6
  279.2 1.5 reshape_squeeze.7
  280.6 2.0 copy.19
  282.6 2.3 rev.15
  284.9 41.6 %while.15 = (s32[]{:T(128)}, f32[512,2,2]{0,2,1:T(2,128)S(1)}, f32[512,2,2]{0,2,1:T(2,128)S(1)}, f32[512,2,2,128]{0,3,2,1:T(8,128)}, s32[4,512]{1,0:T(4,128)S(1)...) while((s32[]{:T(128)}, f32[512,2,2]{0,2,1:T(2,128)S(1)}, ...), condition=%wide.region_4.5_spmd.clone, body=%wide.region_1.4_spmd.clone.sunk | while | flops 551300096 | bytes 42094316 | solution.py:118
  284.9 0.5 fusion.61
  285.5 2.9 fusion.62
  288.4 3.3 fusion.64
  291.8 2.5 fusion.66
  294.3 0.9 copy-done.3
  295.3 0.5 fusion.61
  295.9 2.9 fusion.62
  298.8 3.3 fusion.64
  302.1 0.2 copy-done
  302.3 2.5 fusion.66
  304.8 0.9 copy-done.3
  305.8 0.5 fusion.61
  306.3 2.9 fusion.62
  309.2 3.3 fusion.64
  312.7 2.5 fusion.66
  315.2 0.9 copy-done.3
  316.2 0.5 fusion.61
  316.7 2.9 fusion.62
  319.6 3.3 fusion.64
  323.1 2.5 fusion.66
  325.6 0.9 copy-done.3
  326.5 1.4 divide_convert_fusion
  328.1 8.5 %collective-permute-done.3 = bf16[512,512]{0,1:T(8,128)(2,1)S(1)} collective-permute-done((bf16[512,512]{0,1:T(8,128)(2,1)S(1)}, bf16[512,512]{0,1:T(8,128)(2,1)S(1)}, u32[]{:S(2)}, u32[]{:S(2)}) %collective-permute-start.3) | collective-permute-done | bytes 524320 | tf_op jit(solution)/shard_map/ppermute | solution.py:128
  336.6 8.6 %collective-permute-done.4 = bf16[512,512]{0,1:T(8,128)(2,1)S(1)} collective-permute-done((bf16[512,512]{0,1:T(8,128)(2,1)S(1)}, bf16[512,512]{0,1:T(8,128)(2,1)S(1)}, u32[]{:S(2)}, u32[]{:S(2)}) %collective-permute-start.4) | collective-permute-done | bytes 524320 | tf_op jit(solution)/shard_map/ppermute | solution.py:128
  345.2 8.6 %collective-permute-done.5 = bf16[512,512]{0,1:T(8,128)(2,1)S(1)} collective-permute-done((bf16[512,512]{0,1:T(8,128)(2,1)S(1)}, bf16[512,512]{0,1:T(8,128)(2,1)S(1)}, u32[]{:S(2)}, u32[]{:S(2)}) %collective-permute-start.5) | collective-permute-done | bytes 524320 | tf_op jit(solution)/shard_map/ppermute | solution.py:128
  353.8 0.8 constant_dynamic-update-slice_fusion.7
  354.6 0.8 constant_dynamic-update-slice_fusion.6
  355.4 0.9 constant_dynamic-update-slice_fusion.5
  356.3 0.8 constant_dynamic-update-slice_fusion.4
  357.1 0.8 constant_dynamic-update-slice_fusion.3
  357.9 0.8 constant_dynamic-update-slice_fusion.2
  358.7 0.9 constant_dynamic-update-slice_fusion.1
  359.6 0.9 constant_dynamic-update-slice_fusion
  360.5 1.1 all-gather.15.cloned.1.call-done
  361.6 6.9 %fusion.34 = bf16[512,1152]{1,0:T(8,128)(2,1)} fusion(bf16[2048,1152]{1,0:T(8,128)(2,1)} %all-gather.15.cloned.1.call-done, bf16[512,1152]{1,0:T(8,128)(2,1)S(1)} %copy-done.1, bf16[512,4096]{0,1:T(8,128)(2,1)} %constant_dynamic-update-slice_fusion, s32[]{:T(128)S(6)} %select_n.22), kind=kOutput, calls=%fused_computation.44 | convolution fusion | flops 2417688576 | bytes 9175044 | tf_op jit(solution)/shard_map/dot_general | solution.py:133
  (78 shorter events, 2.2 us)
Async XLA Ops:
  6.5 42.6 %all-gather.7.cloned.1.call-start = ((), (), s32[]{:S(2)}) async-start(), calls=%async_computation | async-start | bytes 5898240 | tf_op jit(solution)/shard_map/all_gather | solution.py:43
  6.5 94.6 %copy-start.5 = (f32[4608]{0:T(1024)S(1)}, f32[4608]{0:T(1024)}, u32[]{:S(2)}) copy-start(f32[4608]{0:T(1024)} %param.10) | copy-start | bytes 55300
  7.3 93.9 %all-gather.9.cloned.1.call-start = ((), (), s32[]{:S(2)}) async-start(), calls=%async_computation.1 | async-start | bytes 2949120 | tf_op jit(solution)/shard_map/all_gather | solution.py:48
  8.0 144.1 %all-gather.11.cloned.1.call-start = ((), (), s32[]{:S(2)}) async-start(), calls=%async_computation.2 | async-start | bytes 2949120 | tf_op jit(solution)/shard_map/all_gather | solution.py:49
  8.7 259.5 %all-gather.13.cloned.1.call-start = ((), (), s32[]{:S(2)}) async-start(), calls=%async_computation.3 | async-start | bytes 5898240 | tf_op jit(solution)/shard_map/all_gather | solution.py:47
  9.3 352.3 %all-gather.15.cloned.1.call-start = ((), (), s32[]{:S(2)}) async-start(), calls=%async_computation.4 | async-start | bytes 5898240 | tf_op jit(solution)/shard_map/all_gather | solution.py:135
  106.3 86.0 %copy-start.4 = (s32[512]{0:T(512)S(1)}, s32[512]{0:T(512)}, u32[]{:S(2)}) copy-start(s32[512]{0:T(512)} %param.15) | copy-start | bytes 6148
  156.7 22.1 %collective-permute-start = (bf16[2,512,256]{2,1,0:T(8,128)(2,1)S(1)}, bf16[2,512,256]{2,1,0:T(8,128)(2,1)S(1)}, u32[]{:S(2)}, u32[]{:S(2)}) collective-permute-start(bf16[2,512,256]{2,1,0:T(8,128)(2,1)S(1)} %pad_maximum_fusion), channel_id=1, source_target_pairs={{0,4},{4,8},{8,12},{1,5},{5,9},{9,13},{2,6},{6,10},{10,14},{3,7},{... | collective-permute-start | bytes 1572872 | tf_op jit(solution)/shard_map/ppermute | solution.py:16
  178.9 59.1 %collective-permute-start.1 = (bf16[2,512,256]{2,1,0:T(8,128)(2,1)S(1)}, bf16[2,512,256]{2,1,0:T(8,128)(2,1)S(1)}, u32[]{:S(2)}, u32[]{:S(2)}) collective-permute-start(bf16[2,512,256]{2,1,0:T(8,128)(2,1)S(1)} %collective-permute-done), channel_id=1, source_target_pairs={{0,4},{4,8},{8,12},{1,5},{5,9},{9,13},{2,6},{6,10},{10,14},{3,7},{... | collective-permute-start | bytes 1572872 | tf_op jit(solution)/shard_map/ppermute | solution.py:16
  238.0 38.2 %collective-permute-start.2 = (bf16[2,512,256]{2,1,0:T(8,128)(2,1)S(1)}, bf16[2,512,256]{2,1,0:T(8,128)(2,1)}, u32[]{:S(2)}, u32[]{:S(2)}) collective-permute-start(bf16[2,512,256]{2,1,0:T(8,128)(2,1)S(1)} %collective-permute-done.1), channel_id=1, source_target_pairs={{0,4},{4,8},{8,12},{1,5},{5,9},{9,13},{2,6},{6,10},{10,14},{3,7},{... | collective-permute-start | bytes 1572872 | tf_op jit(solution)/shard_map/ppermute | solution.py:16
  285.5 6.2 %copy-start.2 = (f32[512,2,2,128]{0,3,2,1:T(8,128)S(1)}, f32[512,2,2,128]{0,3,2,1:T(8,128)}, u32[]{:S(2)}) copy-start(f32[512,2,2,128]{0,3,2,1:T(8,128)} %get-tuple-element.235) | copy-start | bytes 3145732 | tf_op jit(solution)/shard_map/while
  288.4 3.5 copy-start
  294.3 1.0 copy-start.3
  295.9 6.2 %copy-start.2 = (f32[512,2,2,128]{0,3,2,1:T(8,128)S(1)}, f32[512,2,2,128]{0,3,2,1:T(8,128)}, u32[]{:S(2)}) copy-start(f32[512,2,2,128]{0,3,2,1:T(8,128)} %get-tuple-element.235) | copy-start | bytes 3145732 | tf_op jit(solution)/shard_map/while
  298.7 3.5 copy-start
  304.8 1.0 copy-start.3
  306.3 6.2 %copy-start.2 = (f32[512,2,2,128]{0,3,2,1:T(8,128)S(1)}, f32[512,2,2,128]{0,3,2,1:T(8,128)}, u32[]{:S(2)}) copy-start(f32[512,2,2,128]{0,3,2,1:T(8,128)} %get-tuple-element.235) | copy-start | bytes 3145732 | tf_op jit(solution)/shard_map/while
  309.2 3.5 copy-start
  315.2 1.0 copy-start.3
  316.7 6.2 %copy-start.2 = (f32[512,2,2,128]{0,3,2,1:T(8,128)S(1)}, f32[512,2,2,128]{0,3,2,1:T(8,128)}, u32[]{:S(2)}) copy-start(f32[512,2,2,128]{0,3,2,1:T(8,128)} %get-tuple-element.235) | copy-start | bytes 3145732 | tf_op jit(solution)/shard_map/while
  319.6 3.5 copy-start
  325.6 1.0 copy-start.3
  327.9 8.7 %collective-permute-start.3 = (bf16[512,512]{0,1:T(8,128)(2,1)S(1)}, bf16[512,512]{0,1:T(8,128)(2,1)S(1)}, u32[]{:S(2)}, u32[]{:S(2)}) collective-permute-start(bf16[512,512]{0,1:T(8,128)(2,1)S(1)} %bitcast.66), channel_id=1, source_target_pairs={{0,1},{1,2},{2,3},{3,0},{4,5},{5,6},{6,7},{7,4},{8,9},{9,10},{10,1... | collective-permute-start | bytes 1572872 | tf_op jit(solution)/shard_map/ppermute | solution.py:128
  336.6 8.6 %collective-permute-start.4 = (bf16[512,512]{0,1:T(8,128)(2,1)S(1)}, bf16[512,512]{0,1:T(8,128)(2,1)S(1)}, u32[]{:S(2)}, u32[]{:S(2)}) collective-permute-start(bf16[512,512]{0,1:T(8,128)(2,1)S(1)} %collective-permute-done.3), channel_id=1, source_target_pairs={{0,1},{1,2},{2,3},{3,0},{4,5},{5,6},{6,7},{7,4},{8,9},{9,10},{10,1... | collective-permute-start | bytes 1572872 | tf_op jit(solution)/shard_map/ppermute | solution.py:128
  345.2 8.6 %collective-permute-start.5 = (bf16[512,512]{0,1:T(8,128)(2,1)S(1)}, bf16[512,512]{0,1:T(8,128)(2,1)S(1)}, u32[]{:S(2)}, u32[]{:S(2)}) collective-permute-start(bf16[512,512]{0,1:T(8,128)(2,1)S(1)} %collective-permute-done.4), channel_id=1, source_target_pairs={{0,1},{1,2},{2,3},{3,0},{4,5},{5,6},{6,7},{7,4},{8,9},{9,10},{10,1... | collective-permute-start | bytes 1572872 | tf_op jit(solution)/shard_map/ppermute | solution.py:128
  345.2 16.4 %copy-start.1 = (bf16[512,1152]{1,0:T(8,128)(2,1)S(1)}, bf16[512,1152]{1,0:T(8,128)(2,1)}, u32[]{:S(2)}) copy-start(bf16[512,1152]{1,0:T(8,128)(2,1)} %param.9) | copy-start | bytes 3538948
Sparse Core Ops, SparseCore 0:
  8.9 40.1 all-gather.6
  50.7 50.4 all-gather.8
  102.8 49.2 all-gather.10
  153.5 114.6 all-gather.12
  269.6 91.9 all-gather.14
